TPU v7x, 32 devices: a whole 2x2x4 slice. The times are simulated.
32 devices in a mesh: groups: 2 (over y), tensor: 16 (over z, x, core).
Axes of the slice: x: 2, y: 2, z: 4, core: 2. Of those that a mesh axis runs over, the one named last changes fastest.
Arguments:
- inputs: bfloat16 [256, 14336], P('groups', 'tensor'), parts along dimension 0, may hold values from -6 to 6
- base_weight: bfloat16 [14336, 8192], P('tensor')
- cache_shrink: bfloat16 [8, 16, 14336], P('groups', None, 'tensor'), parts along dimension 0
- cache_expand: bfloat16 [8, 16, 8192], P('groups', None, 'tensor'), parts along dimension 0, may hold values from -0.8984375 to 0.8984375
- cache_magnitude: bfloat16 [8, 8192], P('groups', 'tensor'), parts along dimension 0, may hold values from 0.5 to 2
- store_shrink: bfloat16 [64, 16, 14336], P(('groups', 'tensor')), parts along dimension 0
- store_expand: bfloat16 [64, 16, 8192], P(('groups', 'tensor')), parts along dimension 0, may hold values from -0.8984375 to 0.8984375
- store_magnitude: bfloat16 [64, 8192], P(('groups', 'tensor')), parts along dimension 0, may hold values from 0.5 to 2
- tile_adapter: int32 [16], P('groups'), parts along dimension 0, may hold values from 0 to 31, as said below
- row_adapter: int32 [256], P('groups'), parts along dimension 0, may hold values from 0 to 31, as said below
Outputs:
- adapted: bfloat16 [256, 8192], P('groups', 'tensor'), parts along dimension 0
There are 2 independent parts, one for each index of `groups`. A program takes and returns all parts, laid end to end along the dimension named above; an argument that names none is the same for every part. Nothing has to cross between parts.
Inputs may be any that keep to these rules, and one draw needn't show every extreme that they name: `tile_adapter`: 8 different adapter ids; adapters 2j and 2j + 1 are the entries of store_shrink, store_expand and store_magnitude held by tensor index j; the last 4 ids lie on 4 different tensor indices, so no index holds more than one of them. `row_adapter`: every row's id is one of tile_adapter's, and every tile has at least one row.
All inputs are finite; a program needn't handle non-finite values.
Results may differ from a plain program's by a relative error of at most 0.0004.
Values may be sent and summed in bfloat16 or wider, within the bound.
A program may use at most 128 MiB of HBM per device.

v0:
```python
import jax
import jax.numpy as jnp
from jax import lax
from jax.sharding import PartitionSpec as P

ADAPTER_SCALING = 2.0


def local(
    inputs,
    base_weight,
    cache_shrink,
    cache_expand,
    cache_magnitude,
    store_shrink,
    store_expand,
    store_magnitude,
    tile_adapter,
    row_adapter,
):
    highest_precision = lax.Precision.HIGHEST
    position = lax.axis_index("tensor")
    slot_count = store_shrink.shape[0]
    resident = cache_shrink.shape[0]
    new_ids = tile_adapter[resident:]
    owners = new_ids // slot_count
    owned = owners == position
    chosen = jnp.sum(jnp.where(owned, new_ids % slot_count, 0))
    present = jnp.any(owned)

    def select_piece(stored):
        segment = lax.dynamic_index_in_dim(stored, chosen, 0, keepdims=True)
        return jnp.where(present, segment, jnp.zeros_like(segment))

    sent_shrink = select_piece(store_shrink)
    sent_expand = select_piece(store_expand)
    sent_magnitude = select_piece(store_magnitude)[:, None, :]
    got_shrink, got_expand, got_magnitude = (
        lax.all_to_all(sent_shrink, "tensor", split_axis=2, concat_axis=0, tiled=True),
        lax.all_to_all(sent_expand, "tensor", split_axis=2, concat_axis=0, tiled=True),
        lax.all_to_all(sent_magnitude, "tensor", split_axis=2, concat_axis=0, tiled=True),
    )
    down_factor = jnp.concatenate([cache_shrink, jnp.take(got_shrink, owners, axis=0)], 0)
    expand = jnp.concatenate([cache_expand, jnp.take(got_expand, owners, axis=0)], 0)
    magnitude = jnp.concatenate(
        [cache_magnitude, jnp.take(got_magnitude, owners, axis=0)[:, 0, :]], 0
    ).astype(jnp.float32)
    tile_count = down_factor.shape[0]
    rank_size = down_factor.shape[1]
    row_count = inputs.shape[0]
    own_width = expand.shape[2]
    flat_shrink = down_factor.reshape(tile_count * rank_size, down_factor.shape[2])
    row_tile = (row_adapter[:, None] == tile_adapter[None, :]).astype(jnp.float32)
    projected = lax.dot_general(
        inputs, flat_shrink, (((1,), (1,)), ((), ())), preferred_element_type=jnp.float32
    )
    low_part = jnp.sum(
        row_tile[:, :, None] * projected.reshape(row_count, tile_count, rank_size), axis=1
    )
    base_part = jnp.dot(inputs, base_weight, preferred_element_type=jnp.float32)
    expand_wide = expand.astype(jnp.float32)
    col_part = jnp.sum(jnp.square(base_weight.astype(jnp.float32)), axis=0)
    partial_gram_matrix = jnp.einsum(
        "aig,ahg->aih", down_factor, down_factor, preferred_element_type=jnp.float32
    )
    low, gram_sum, column_square_sums = lax.psum(
        (low_part, partial_gram_matrix, col_part), "tensor"
    )
    cross = lax.psum_scatter(
        lax.dot_general(
            base_weight, flat_shrink, (((0,), (1,)), ((), ())), preferred_element_type=jnp.float32
        ),
        "tensor",
        scatter_dimension=0,
        tiled=True,
    ).reshape(own_width, tile_count, rank_size)
    frozen_output = lax.psum_scatter(base_part, "tensor", scatter_dimension=1, tiled=True)
    local_column_slice = lax.dynamic_slice_in_dim(
        column_square_sums, position * own_width, own_width
    )
    linear_term = jnp.einsum("dtr,trd->td", cross, expand_wide, precision=highest_precision)
    quadratic_term = jnp.sum(
        expand_wide
        * jnp.einsum("trq,tqd->trd", gram_sum, expand_wide, precision=highest_precision),
        axis=1,
    )
    squared_norm = (
        local_column_slice[None, :]
        + 2.0 * ADAPTER_SCALING * linear_term
        + ADAPTER_SCALING * ADAPTER_SCALING * quadratic_term
    )
    factor = magnitude / jnp.sqrt(squared_norm)
    spread = (row_tile[:, :, None] * low[:, None, :]).reshape(row_count, tile_count * rank_size)
    low_rank_update = jnp.dot(
        spread, expand_wide.reshape(tile_count * rank_size, own_width), precision=highest_precision
    )
    row_multiplier = jnp.dot(row_tile, factor, precision=highest_precision)
    return (row_multiplier * (frozen_output + ADAPTER_SCALING * low_rank_update)).astype(
        jnp.bfloat16
    )


def solution(mesh):
    in_specs = (
        P("groups", "tensor"),
        P("tensor", None),
        P("groups", None, "tensor"),
        P("groups", None, "tensor"),
        P("groups", "tensor"),
        P(("groups", "tensor"), None, None),
        P(("groups", "tensor"), None, None),
        P(("groups", "tensor"), None),
        P("groups"),
        P("groups"),
    )
    out_specs = P("groups", "tensor")
    return jax.shard_map(local, mesh=mesh, in_specs=in_specs, out_specs=out_specs, check_vma=False)
```

profile of v0, /device:TPU:0, one launch (start us, length us, event | category | flops | bytes accessed | tf_op | source)
XLA Modules:
  0.0 495.3 jit_solution(12244749328627004139)
XLA Ops:
  6.5 0.0 copy-start
  6.5 0.0 reduce-scatter.5.cloned.1.call-start
  6.5 9.8 %fusion.31 = f32[128,8192]{1,0:T(8,128)} fusion(bf16[128,896]{1,0:T(8,128)(2,1)} %param.10, bf16[896,8192]{1,0:T(8,128)(2,1)} %param.11), kind=kOutput, calls=%fused_computation.65 | convolution fusion | flops 1879048192 | bytes 19103744 | tf_op jit(solution)/shard_map/dot_general | solution.py:60
  16.4 0.0 reduce-scatter.5.cloned.1.call-update
  16.4 0.0 copy-done.7
  16.4 0.1 compare_and_fusion
  16.5 0.7 compare_select_fusion
  19.2 0.0 copy-done
  19.2 11.4 %copy.32 = bf16[1,16,14336]{1,0,2:T(2,128)(2,1)} copy(bf16[1,16,14336]{2,1,0:T(8,128)(2,1)S(1)} %constant_dynamic-slice_fusion.1) | data formatting | bytes 917504
  30.6 0.6 compare_reduce_fusion
  31.2 9.9 %fusion.29 = bf16[14336,1,16]{2,1,0:T(2,128)(2,1)} fusion(bf16[1,16,14336]{1,0,2:T(2,128)(2,1)} %copy.32, pred[]{:T(512)} %compare_reduce_fusion), kind=kLoop, calls=%fused_computation.62 | loop fusion | flops 229376 | bytes 917505
  41.2 0.5 broadcast.106
  41.7 79.7 %reduce.5 = bf16[14336,16]{1,0:T(8,128)(2,1)} reduce(bf16[14336,1,16]{2,1,0:T(2,128)(2,1)} %fusion.29, bf16[]{:T(256)} %broadcast.106), dimensions={1}, to_apply=%fusion.29.reduce_sub_computation | reduce | bytes 917506
  121.4 6.4 %reshape.97 = bf16[16,2,7168]{2,1,0:T(2,128)(2,1)} reshape(bf16[14336,16]{1,0:T(8,128)(2,1)} %reduce.5) | data formatting | bytes 917504
  127.8 7.4 %all-to-all-start.1 = ((bf16[16,2,7168]{2,1,0:T(2,128)(2,1)}), bf16[16,2,7168]{2,1,0:T(2,128)(2,1)S(1)}, u32[]{:S(2)}, u32[]{:S(2)}) async-start(bf16[16,2,7168]{2,1,0:T(2,128)(2,1)} %reshape.97), calls=%async_computation.1 | async-start | bytes 917504 | tf_op jit(solution)/shard_map/all_to_all | solution.py:39
  135.1 0.2 reduce-scatter.3.cloned.1.call-start
  135.4 0.0 copy-start.5
  135.4 13.0 %all-to-all-done.1 = bf16[16,2,7168]{2,1,0:T(2,128)(2,1)S(1)} async-done(((bf16[16,2,7168]{2,1,0:T(2,128)(2,1)}), bf16[16,2,7168]{2,1,0:T(2,128)(2,1)S(1)}, u32[]{:S(2)}, u32[]{:S(2)}) %all-to-all-start.1) | async-done | bytes 458784 | tf_op jit(solution)/shard_map/all_to_all | solution.py:39
  148.4 9.3 %reshape.98 = bf16[14336,1,16]{2,1,0:T(2,128)(2,1)} reshape(bf16[16,2,7168]{2,1,0:T(2,128)(2,1)S(1)} %all-to-all-done.1) | data formatting | bytes 917504
  157.6 13.5 %copy.21 = bf16[1,16,14336]{2,1,0:T(8,128)(2,1)S(1)} copy(bf16[1,16,14336]{1,0,2:T(2,128)(2,1)} %bitcast.54) | data formatting | bytes 917504 | tf_op jit(solution)/shard_map/all_to_all | solution.py:39
  171.2 0.6 gather_fusion.1
  171.8 0.1 broadcast_select_fusion.2
  171.9 0.0 copy-done.5
  171.9 0.0 copy-start.6
  171.9 9.5 %convolution_bitcast_fusion = f32[8192,128]{0,1:T(8,128)} fusion(bf16[128,896]{1,0:T(8,128)(2,1)S(1)} %bitcast.57, bf16[896,8192]{1,0:T(8,128)(2,1)} %param.11), kind=kOutput, calls=%fused_computation.5 | convolution fusion | flops 1879048192 | bytes 19103744 | tf_op jit(solution)/shard_map/dot_general | solution.py:70
  181.4 0.0 reduce-scatter.3.cloned.1.call-update
  181.4 0.0 copy-done.6
  181.4 0.7 fusion.5
  182.1 6.8 %copy.19 = bf16[1,1,8192]{1,0,2:T(2,128)(2,1)} copy(bf16[1,1,8192]{2,1,0:T(2,128)(2,1)S(1)} %fusion.5) | data formatting | bytes 32768 | tf_op jit(solution)/shard_map/broadcast_in_dim | solution.py:37
  188.9 62.6 %reduce.6 = bf16[8192]{0:T(1024)(128)(2,1)S(1)} reduce(bf16[8192,1,1]{2,1,0:T(2,128)(2,1)} %bitcast.55, bf16[]{:T(256)} %broadcast.106), dimensions={1,2}, to_apply=%bitcast.38.reduce_sub_computation | reduce | bytes 32770
  251.5 0.6 reshape.99
  252.1 4.1 all-to-all-start
  256.2 0.0 copy-done.4
  256.3 6.7 %copy.33 = bf16[1,16,8192]{1,0,2:T(2,128)(2,1)} copy(bf16[1,16,8192]{2,1,0:T(8,128)(2,1)S(1)} %constant_dynamic-slice_fusion) | data formatting | bytes 524288
  263.0 8.3 %multiply_reduce_fusion = f32[8192]{0:T(1024)S(1)} fusion(bf16[896,8192]{1,0:T(8,128)(2,1)} %param.11), kind=kLoop, calls=%fused_computation.3 | loop fusion | flops 22011904 | bytes 14712832 | tf_op jit(solution)/shard_map/reduce_sum | solution.py:62
  271.2 0.0 copy-start.9
  271.3 6.8 %fusion.30 = bf16[8192,1,16]{2,1,0:T(2,128)(2,1)} fusion(bf16[1,16,8192]{1,0,2:T(2,128)(2,1)} %copy.33, pred[]{:T(512)} %compare_reduce_fusion), kind=kLoop, calls=%fused_computation.64 | loop fusion | flops 131072 | bytes 524289
  278.0 0.0 copy-done.9
  278.0 0.1 compare_convert_fusion
  278.1 45.1 %reduce.4 = bf16[8192,16]{1,0:T(8,128)(2,1)S(1)} reduce(bf16[8192,1,16]{2,1,0:T(2,128)(2,1)} %fusion.30, bf16[]{:T(256)} %broadcast.106), dimensions={1}, to_apply=%fusion.30.reduce_sub_computation | reduce | bytes 524290
  323.3 2.8 reshape.95
  326.1 0.0 all-to-all-done
  326.1 7.6 %all-to-all-start.2 = ((bf16[16,2,4096]{2,1,0:T(2,128)(2,1)}), bf16[16,2,4096]{2,1,0:T(2,128)(2,1)S(1)}, u32[]{:S(2)}, u32[]{:S(2)}) async-start(bf16[16,2,4096]{2,1,0:T(2,128)(2,1)} %reshape.95), calls=%async_computation.3 | async-start | bytes 524288 | tf_op jit(solution)/shard_map/all_to_all | solution.py:40
  333.7 8.4 %reshape.100 = bf16[8192,1,1]{2,1,0:T(2,128)(2,1)} reshape(bf16[16,2,256]{2,1,0:T(2,128)(2,1)S(1)} %all-to-all-done) | data formatting | bytes 32768
  342.0 62.1 %bitcast_reduce_fusion = bf16[8192]{0:T(1024)(128)(2,1)S(1)} fusion(bf16[8192,1,1]{2,1,0:T(2,128)(2,1)} %reshape.100), kind=kLoop, calls=%fused_computation.63 | loop fusion | bytes 32768 | tf_op jit(solution)/shard_map/all_to_all | solution.py:41
  404.2 0.6 gather_fusion
  404.7 0.1 broadcast_select_fusion.5
  404.8 0.0 all-to-all-done.2
  404.8 7.6 %reshape.96 = bf16[8192,1,16]{2,1,0:T(2,128)(2,1)} reshape(bf16[16,2,4096]{2,1,0:T(2,128)(2,1)S(1)} %all-to-all-done.2) | data formatting | bytes 524288
  412.4 7.9 %copy.24 = bf16[1,16,8192]{2,1,0:T(8,128)(2,1)S(1)} copy(bf16[1,16,8192]{1,0,2:T(2,128)(2,1)} %bitcast.56) | data formatting | bytes 524288 | tf_op jit(solution)/shard_map/all_to_all | solution.py:40
  420.3 0.6 gather_fusion.2
  420.9 0.1 broadcast_select_fusion.3
  420.9 0.2 fusion.28
  421.1 0.0 copy-done.2
  421.1 0.2 fusion.32
  421.4 62.8 %all-reduce = (f32[128,16]{0,1:T(8,128)S(1)}, f32[8,16,16]{2,1,0:T(8,128)S(1)}, f32[8192]{0:T(1024)S(1)}) all-reduce(f32[128,16]{0,1:T(8,128)S(1)} %multiply_reduce_fusion.2, f32[8,16,16]{2,1,0:T(8,128)S(1)} %fusion.28, f32[8192]{0:T(1024)S(1)} %multiply_reduce_fusion), channel_id=1, replica_groups=mesh['groups'=2,'tensor'=16] {'tensor'}, use_global_device_ids=true, to_apply=%region_9.10 | all-reduce | flops 12288 | bytes 98304 | tf_op jit(solution)/shard_map/psum | solution.py:66
  484.3 0.1 dynamic_slice.16
  484.4 0.3 fusion.3
  484.6 0.0 reduce-scatter.5.cloned.1.call-done
  484.7 1.3 fusion.1
  485.9 0.0 reduce-scatter.3.cloned.1.call-done
  486.0 1.0 multiply_reduce_fusion.1
  487.0 1.0 fusion.2
  488.0 0.0 copy-done.1
  (16 shorter events, 0.2 us)
Async XLA Ops:
  6.5 12.6 %copy-start = (bf16[2,16,14336]{2,1,0:T(8,128)(2,1)S(1)}, bf16[2,16,14336]{2,1,0:T(8,128)(2,1)}, u32[]{:S(2)}) copy-start(bf16[2,16,14336]{2,1,0:T(8,128)(2,1)} %param.15) | copy-start | bytes 2752516
  6.5 9.9 %copy-start.7 = (s32[8]{0:T(128)S(1)}, s32[8]{0:T(128)}, u32[]{:S(2)}) copy-start(s32[8]{0:T(128)} %param.18) | copy-start | bytes 100
  6.5 478.1 %reduce-scatter.5.cloned.1.call-start = ((), (), s32[]{:S(2)}) async-start(), calls=%async_computation.6 | async-start | bytes 4456448 | tf_op jit(solution)/shard_map/reduce_scatter | solution.py:77
  127.8 20.6 %all-to-all-start.1 = ((bf16[16,2,7168]{2,1,0:T(2,128)(2,1)}), bf16[16,2,7168]{2,1,0:T(2,128)(2,1)S(1)}, u32[]{:S(2)}, u32[]{:S(2)}) async-start(bf16[16,2,7168]{2,1,0:T(2,128)(2,1)} %reshape.97), calls=%async_computation.1 | async-start | bytes 917504 | tf_op jit(solution)/shard_map/all_to_all | solution.py:39
  135.1 350.8 %reduce-scatter.3.cloned.1.call-start = ((), (), s32[]{:S(2)}) async-start(), calls=%async_computation.5 | async-start | bytes 4456448 | tf_op jit(solution)/shard_map/reduce_scatter | solution.py:69
  135.4 36.5 %copy-start.5 = (bf16[4,16,896]{2,1,0:T(8,128)(2,1)S(1)}, bf16[4,16,896]{2,1,0:T(8,128)(2,1)}, u32[]{:S(2)}) copy-start(bf16[4,16,896]{2,1,0:T(8,128)(2,1)} %param.12) | copy-start | bytes 344068
  171.9 9.5 %copy-start.6 = (bf16[2,8192]{1,0:T(2,128)(2,1)S(1)}, bf16[2,8192]{1,0:T(2,128)(2,1)}, u32[]{:S(2)}) copy-start(bf16[2,8192]{1,0:T(2,128)(2,1)} %param.17) | copy-start | bytes 98308
  181.4 74.9 %copy-start.4 = (bf16[2,16,8192]{2,1,0:T(8,128)(2,1)S(1)}, bf16[2,16,8192]{2,1,0:T(8,128)(2,1)}, u32[]{:S(2)}) copy-start(bf16[2,16,8192]{2,1,0:T(8,128)(2,1)} %param.16) | copy-start | bytes 1572868
  252.1 74.0 %all-to-all-start = ((bf16[16,2,256]{2,1,0:T(2,128)(2,1)}), bf16[16,2,256]{2,1,0:T(2,128)(2,1)S(1)}, u32[]{:S(2)}, u32[]{:S(2)}) async-start(bf16[16,2,256]{2,1,0:T(2,128)(2,1)} %reshape.99), calls=%async_computation | async-start | bytes 32768 | tf_op jit(solution)/shard_map/all_to_all | solution.py:41
  271.2 6.8 %copy-start.9 = (s32[128]{0:T(128)S(1)}, s32[128]{0:T(128)}, u32[]{:S(2)}) copy-start(s32[128]{0:T(128)} %param.19) | copy-start | bytes 1540
  326.1 78.7 %all-to-all-start.2 = ((bf16[16,2,4096]{2,1,0:T(2,128)(2,1)}), bf16[16,2,4096]{2,1,0:T(2,128)(2,1)S(1)}, u32[]{:S(2)}, u32[]{:S(2)}) async-start(bf16[16,2,4096]{2,1,0:T(2,128)(2,1)} %reshape.95), calls=%async_computation.3 | async-start | bytes 524288 | tf_op jit(solution)/shard_map/all_to_all | solution.py:40
  342.0 79.1 %copy-start.2 = (bf16[128,896]{1,0:T(8,128)(2,1)S(1)}, bf16[128,896]{1,0:T(8,128)(2,1)}, u32[]{:S(2)}) copy-start(bf16[128,896]{1,0:T(8,128)(2,1)} %param.10) | copy-start | bytes 688132
  342.0 142.3 %copy-start.3 = (bf16[4,16,512]{2,1,0:T(8,128)(2,1)S(1)}, bf16[4,16,512]{2,1,0:T(8,128)(2,1)}, u32[]{:S(2)}) copy-start(bf16[4,16,512]{2,1,0:T(8,128)(2,1)} %param.13) | copy-start | bytes 196612
  342.0 146.0 %copy-start.1 = (bf16[2,16,14336]{2,1,0:T(8,128)(2,1)S(1)}, bf16[2,16,14336]{2,1,0:T(8,128)(2,1)}, u32[]{:S(2)}) copy-start(bf16[2,16,14336]{2,1,0:T(8,128)(2,1)} %param.15) | copy-start | bytes 2752516
  404.1 82.9 %copy-start.8 = (bf16[4,512]{1,0:T(4,128)(2,1)S(1)}, bf16[4,512]{1,0:T(4,128)(2,1)}, u32[]{:S(2)}) copy-start(bf16[4,512]{1,0:T(4,128)(2,1)} %param.14) | copy-start | bytes 12292
Sparse Core Ops, SparseCore 0:
  16.5 75.1 reduce-scatter.4
  181.5 71.5 reduce-scatter.2
where the time goes:
time: 504 us; the launch traced here: 495 us
  other arithmetic  216 us (43%)
  local copies, waits for them, and re-layouts  146 us (29%)
  blocking collectives  62.8 us (12%)
  matrix products  22.3 us (4%)
  starting transfers between devices  19.3 us (4%)
  between operations  16.1 us (3%)
  waiting for transfers between devices  13.1 us (3%)
    unnamed x5, other arithmetic  204 us
    psum x1, blocking collectives, local(): lax.psum((low_part, partial_gram_matrix, col_part), 'tensor')  62.8 us
    all_to_all x2, local copies, waits for them, and re-layouts, local(): lax.all_to_all(sent_magnitude, 'tensor', split_axis=2, concat_axis=0, til...  62.1 us
    unnamed x29, local copies, waits for them, and re-layouts  53.6 us
    all_to_all x2, local copies, waits for them, and re-layouts, local(): lax.all_to_all(sent_shrink, 'tensor', split_axis=2, concat_axis=0, tiled=...  13.5 us
    all_to_all x1, waiting for transfers between devices, local(): lax.all_to_all(sent_shrink, 'tensor', split_axis=2, concat_axis=0, tiled=...  13 us
  transfers between devices with their start and end apart: 5, of which 1 were waited for; matrix products, arithmetic and copies ran while one was open for 75% of the time, Pallas kernels for 0%

commit v1 on v0

--- a/solution.py
+++ b/solution.py
@@ -1,12 +1,16 @@
+import functools
+
 import jax
 import jax.numpy as jnp
 from jax import lax
+from jax.experimental import pallas as pl
+from jax.experimental.pallas import tpu as pltpu
 from jax.sharding import PartitionSpec as P
 
 ADAPTER_SCALING = 2.0
 
 
-def local(
+def plain_local(
     inputs,
     base_weight,
     cache_shrink,
@@ -100,6 +104,475 @@
     )
 
 
+LAG = 4
+MESH = pl.DeviceIdType.MESH
+
+
+def split3(value):
+    high = value.astype(jnp.bfloat16)
+    rest = value - high.astype(jnp.float32)
+    middle = rest.astype(jnp.bfloat16)
+    low = (rest - middle.astype(jnp.float32)).astype(jnp.bfloat16)
+    return high, middle, low
+
+
+def exact_dot(left, right, dims):
+    return sum(
+        lax.dot_general(part, right, (dims, ((), ())), preferred_element_type=jnp.float32)
+        for part in reversed(split3(left))
+    )
+
+
+def fused_kernel(
+    n,
+    owners_ref,
+    inputs_ref,
+    weight_ref,
+    cache_shrink_ref,
+    cache_expand_ref,
+    cache_magnitude_ref,
+    shrink_ref,
+    expand_ref,
+    magnitude_ref,
+    row_mask_ref,
+    out_ref,
+    weight_buf,
+    got_shrink,
+    got_expand,
+    got_magnitude,
+    flat_shrink,
+    flat_expand,
+    base_pair_out,
+    base_pair_in,
+    base_ring_out,
+    base_ring_in,
+    cross_pair_out,
+    cross_pair_in,
+    cross_ring_out,
+    cross_ring_in,
+    base_sum,
+    cross_sum,
+    small_out,
+    small_in,
+    weight_sem,
+    piece_send,
+    piece_recv,
+    pair_send,
+    pair_recv,
+    ring_send,
+    ring_recv,
+    small_send,
+    small_recv,
+):
+    me = lax.axis_index("tensor")
+    chips = n // 2
+    half = n // 4
+    core = lax.rem(me, 2)
+    chip = lax.div(me, 2)
+    across = lax.rem(chip, 2)
+    along = lax.div(chip, 2)
+    place = along + across * (2 * half - 1 - 2 * along)
+    step = 1 - 2 * core
+
+    def device_at(spot, which):
+        spot = lax.rem(spot + 4 * chips, chips)
+        side = lax.div(spot, half)
+        depth = spot + side * (2 * half - 1 - 2 * spot)
+        return (depth * 2 + side) * 2 + which
+
+    partner = device_at(place, 1 - core)
+    following = device_at(place + step, core)
+    rows, hidden = inputs_ref.shape
+    width = out_ref.shape[1]
+    rank = shrink_ref.shape[0]
+    new = owners_ref.shape[0]
+    resident_rows = cache_shrink_ref.shape[0]
+    tile_rows = flat_shrink.shape[0]
+    tiles = tile_rows // rank
+
+    def weight_copy(slot):
+        turn = lax.div(slot, 2)
+        own = lax.rem(slot, 2)
+        spot = place + (1 - 2 * own) * step * (1 + turn)
+        which = own * core + (1 - own) * (1 - core)
+        block = device_at(spot, which)
+        column = pl.multiple_of(block * width, width)
+        return pltpu.make_async_copy(
+            weight_ref.at[:, pl.ds(column, width)], weight_buf.at[slot], weight_sem.at[slot]
+        )
+
+    def start_weight(slot, carry):
+        weight_copy(slot).start()
+        return carry
+
+    lax.fori_loop(0, n, start_weight, 0)
+
+    barrier = pltpu.get_barrier_semaphore()
+
+    def greet(offset, carry):
+        pl.semaphore_signal(
+            barrier,
+            inc=1,
+            device_id={"tensor": lax.rem(me + offset, n)},
+            device_id_type=MESH,
+        )
+        return carry
+
+    lax.fori_loop(1, n, greet, 0)
+    pl.semaphore_wait(barrier, n - 1)
+
+    def piece_parts(target):
+        shrink_column = pl.multiple_of(target * hidden, 128)
+        expand_column = pl.multiple_of(target * width, 128)
+        return (
+            (shrink_ref.at[:, pl.ds(shrink_column, hidden)], got_shrink),
+            (expand_ref.at[:, pl.ds(expand_column, width)], got_expand),
+            (magnitude_ref.at[target], got_magnitude),
+        )
+
+    def piece_copies(offset):
+        target = lax.rem(me + offset, n)
+        return [
+            pltpu.make_async_remote_copy(
+                src_ref=source,
+                dst_ref=landing.at[me],
+                send_sem=piece_send.at[kind, offset],
+                recv_sem=piece_recv.at[kind, me],
+                device_id={"tensor": target},
+                device_id_type=MESH,
+            )
+            for kind, (source, landing) in enumerate(piece_parts(target))
+        ]
+
+    def start_pieces(offset, carry):
+        for copy in piece_copies(offset):
+            copy.start()
+        return carry
+
+    def piece_sent(offset, carry):
+        for copy in piece_copies(offset):
+            copy.wait_send()
+        return carry
+
+    def own_pieces():
+        return [
+            pltpu.make_async_copy(source, landing.at[me], piece_recv.at[kind, me])
+            for kind, (source, landing) in enumerate(piece_parts(me))
+        ]
+
+    def piece_arrived(sender, carry):
+        for kind, landing in enumerate((got_shrink, got_expand, got_magnitude)):
+            pltpu.make_async_copy(
+                landing.at[sender], landing.at[sender], piece_recv.at[kind, sender]
+            ).wait()
+        return carry
+
+    def pair_copy(chain, turn):
+        source, landing = ((base_pair_out, base_pair_in), (cross_pair_out, cross_pair_in))[chain]
+        return pltpu.make_async_remote_copy(
+            src_ref=source.at[turn],
+            dst_ref=landing.at[turn],
+            send_sem=pair_send.at[chain, turn],
+            recv_sem=pair_recv.at[chain, turn],
+            device_id={"tensor": partner},
+            device_id_type=MESH,
+        )
+
+    def ring_copy(chain, turn):
+        source, landing = ((base_ring_out, base_ring_in), (cross_ring_out, cross_ring_in))[chain]
+        return pltpu.make_async_remote_copy(
+            src_ref=source.at[turn],
+            dst_ref=landing.at[turn],
+            send_sem=ring_send.at[chain, turn],
+            recv_sem=ring_recv.at[chain, turn],
+            device_id={"tensor": following},
+            device_id_type=MESH,
+        )
+
+    def small_copy(offset):
+        return pltpu.make_async_remote_copy(
+            src_ref=small_out,
+            dst_ref=small_in.at[me],
+            send_sem=small_send.at[offset],
+            recv_sem=small_recv.at[me],
+            device_id={"tensor": lax.rem(me + offset, n)},
+            device_id_type=MESH,
+        )
+
+    def squares(slot):
+        chunk = 64
+
+        def add(index, total):
+            part = weight_buf[slot, pl.ds(pl.multiple_of(index * chunk, chunk), chunk), :]
+            part = part.astype(jnp.float32)
+            return total + jnp.sum((part * part).reshape(chunk // 8, 8, width), axis=0)
+
+        return lax.fori_loop(0, hidden // chunk, add, jnp.zeros((8, width), jnp.float32))
+
+    def product(chain, slot):
+        left = (inputs_ref, flat_shrink)[chain]
+        return jnp.dot(left[...], weight_buf[slot], preferred_element_type=jnp.float32)
+
+    def to_partner(chain, turn):
+        slot = 2 * turn
+        out = (base_pair_out, cross_pair_out)[chain]
+        if chain == 0:
+            weight_copy(slot).wait()
+            out[turn, pl.ds(rows, 8), :] = squares(slot)
+        out[turn, pl.ds(0, rows if chain == 0 else tile_rows), :] = product(chain, slot)
+        pair_copy(chain, turn).start()
+
+    def ring_turn(chain, turn):
+        slot = 2 * turn + 1
+        total = (base_sum, cross_sum)[chain]
+        ring_out = (base_ring_out, cross_ring_out)[chain]
+        ring_in = (base_ring_in, cross_ring_in)[chain]
+        pair_in = (base_pair_in, cross_pair_in)[chain]
+        if chain == 0:
+            weight_copy(slot).wait()
+            total[pl.ds(rows, 8), :] = squares(slot)
+        total[pl.ds(0, rows if chain == 0 else tile_rows), :] = product(chain, slot)
+        pair_copy(chain, turn).wait_recv()
+        total[...] += pair_in[turn]
+
+        @pl.when(turn > 0)
+        def _():
+            ring_copy(chain, turn - 1).wait_recv()
+            total[...] += ring_in[turn - 1]
+
+        @pl.when(turn < chips - 1)
+        def _():
+            ring_out[turn] = total[...]
+            ring_copy(chain, turn).start()
+
+    def adapters_ready():
+        lax.fori_loop(0, n, piece_arrived, 0)
+        flat_shrink[pl.ds(0, resident_rows), :] = cache_shrink_ref[...]
+        flat_expand[pl.ds(0, resident_rows), :] = cache_expand_ref[...]
+        for tile in range(new):
+            owner = owners_ref[tile]
+            target = pl.ds(resident_rows + tile * rank, rank)
+            flat_shrink[target, :] = got_shrink[owner]
+            flat_expand[target, :] = got_expand[owner]
+        shrink = flat_shrink[...]
+        contract = (((1,), (1,)), ((), ()))
+        low = lax.dot_general(
+            shrink, inputs_ref[...], contract, preferred_element_type=jnp.float32
+        )
+        gram = lax.dot_general(shrink, shrink, contract, preferred_element_type=jnp.float32)
+        low = jnp.sum((low * row_mask_ref[...]).reshape(tiles, rank, rows), axis=0)
+        gram = jnp.where(tile_mask(), gram, 0.0)
+        gram = jnp.sum(gram.reshape(tiles, rank, tile_rows), axis=0)
+        small_out[pl.ds(0, rank), :] = low
+        small_out[pl.ds(rank, rank), :] = gram
+
+        def send(offset, carry):
+            small_copy(offset).start()
+            return carry
+
+        lax.fori_loop(1, n, send, 0)
+
+    def tile_mask():
+        shape = (tile_rows, tile_rows)
+        first = lax.broadcasted_iota(jnp.int32, shape, 0) // rank
+        second = lax.broadcasted_iota(jnp.int32, shape, 1) // rank
+        return first == second
+
+    to_partner(0, 0)
+    for copy in own_pieces():
+        copy.start()
+    lax.fori_loop(1, n, start_pieces, 0)
+
+    def turn_body(turn, carry):
+        @pl.when(turn < chips - 1)
+        def _():
+            to_partner(0, turn + 1)
+
+        @pl.when(turn < chips)
+        def _():
+            ring_turn(0, turn)
+
+        @pl.when(turn == LAG - 1)
+        def _():
+            adapters_ready()
+            to_partner(1, 0)
+
+        @pl.when((turn >= LAG) & (turn < chips + LAG - 1))
+        def _():
+            to_partner(1, turn - LAG + 1)
+
+        @pl.when(turn >= LAG)
+        def _():
+            ring_turn(1, turn - LAG)
+
+        return carry
+
+    lax.fori_loop(0, chips + LAG, turn_body, 0)
+
+    def add_small(offset, total):
+        sender = lax.rem(me + offset, n)
+        pltpu.make_async_copy(
+            small_in.at[sender], small_in.at[sender], small_recv.at[sender]
+        ).wait()
+        return total + small_in[sender]
+
+    small = lax.fori_loop(1, n, add_small, small_out[...])
+    low = jnp.concatenate([small[:rank]] * tiles, 0)
+    gram = jnp.where(tile_mask(), jnp.concatenate([small[rank:]] * tiles, 0), 0.0)
+    expand = flat_expand[...]
+    wide = expand.astype(jnp.float32)
+    quadratic = exact_dot(gram, expand, ((1,), (0,)))
+    change = jnp.sum(
+        (wide * (cross_sum[...] + quadratic)).reshape(tiles, rank, width), axis=1
+    )
+    column_squares = jnp.sum(base_sum[pl.ds(rows, 8), :], axis=0, keepdims=True)
+    squared_norm = column_squares + 2.0 * ADAPTER_SCALING * change
+    magnitude = jnp.concatenate(
+        [cache_magnitude_ref[...]] + [got_magnitude[owners_ref[t]] for t in range(new)], 0
+    )
+    factor = magnitude / jnp.sqrt(squared_norm)
+    row_mask = row_mask_ref[...]
+    update = exact_dot(low * row_mask, expand, ((0,), (0,)))
+    spread = jnp.broadcast_to(factor[:, None, :], (tiles, rank, width)).reshape(tile_rows, width)
+    pick = lax.broadcasted_iota(jnp.int32, row_mask.shape, 0) % rank == 0
+    pick = jnp.where(pick, row_mask, 0.0).astype(jnp.bfloat16)
+    multiplier = sum(
+        lax.dot_general(
+            pick, part, (((0,), (0,)), ((), ())), preferred_element_type=jnp.float32
+        )
+        for part in reversed(split3(spread))
+    )
+    base = base_sum[pl.ds(0, rows), :]
+    out_ref[...] = (multiplier * (base + ADAPTER_SCALING * update)).astype(out_ref.dtype)
+
+    lax.fori_loop(1, n, piece_sent, 0)
+
+    def small_sent(offset, carry):
+        small_copy(offset).wait_send()
+        return carry
+
+    lax.fori_loop(1, n, small_sent, 0)
+
+    def turn_sent(turn, carry):
+        for chain in range(2):
+            pair_copy(chain, turn).wait_send()
+
+            @pl.when(turn < chips - 1)
+            def _():
+                ring_copy(chain, turn).wait_send()
+
+        return carry
+
+    lax.fori_loop(0, chips, turn_sent, 0)
+
+
+def fused_local(
+    n,
+    inputs,
+    base_weight,
+    cache_shrink,
+    cache_expand,
+    cache_magnitude,
+    store_shrink,
+    store_expand,
+    store_magnitude,
+    tile_adapter,
+    row_adapter,
+):
+    position = lax.axis_index("tensor")
+    slot_count, rank, _ = store_shrink.shape
+    resident, _, hidden = cache_shrink.shape
+    width = cache_expand.shape[2]
+    rows = inputs.shape[0]
+    tiles = tile_adapter.shape[0]
+    tile_rows = tiles * rank
+    owners = tile_adapter[resident:] // slot_count
+    chosen = jnp.sum(
+        jnp.where(owners == position, tile_adapter[resident:] % slot_count, 0)
+    )
+
+    def select(stored):
+        return lax.dynamic_index_in_dim(stored, chosen, 0, keepdims=False)
+
+    row_mask = (jnp.repeat(tile_adapter, rank)[:, None] == row_adapter[None, :]).astype(
+        jnp.float32
+    )
+    chips = n // 2
+    tall = rows + 8
+    vmem = pl.BlockSpec(memory_space=pltpu.VMEM)
+    return pl.pallas_call(
+        functools.partial(fused_kernel, n),
+        out_shape=jax.ShapeDtypeStruct((rows, width), jnp.bfloat16),
+        in_specs=[pl.BlockSpec(memory_space=pltpu.SMEM), vmem, pl.BlockSpec(memory_space=pl.ANY)]
+        + [vmem] * 7,
+        out_specs=vmem,
+        scratch_shapes=[
+            pltpu.VMEM((n, hidden, width), jnp.bfloat16),
+            pltpu.VMEM((n, rank, hidden), jnp.bfloat16),
+            pltpu.VMEM((n, rank, width), jnp.bfloat16),
+            pltpu.VMEM((n, 1, width), jnp.float32),
+            pltpu.VMEM((tile_rows, hidden), jnp.bfloat16),
+            pltpu.VMEM((tile_rows, width), jnp.bfloat16),
+            pltpu.VMEM((chips, tall, width), jnp.float32),
+            pltpu.VMEM((chips, tall, width), jnp.float32),
+            pltpu.VMEM((chips - 1, tall, width), jnp.float32),
+            pltpu.VMEM((chips - 1, tall, width), jnp.float32),
+            pltpu.VMEM((chips, tile_rows, width), jnp.float32),
+            pltpu.VMEM((chips, tile_rows, width), jnp.float32),
+            pltpu.VMEM((chips - 1, tile_rows, width), jnp.float32),
+            pltpu.VMEM((chips - 1, tile_rows, width), jnp.float32),
+            pltpu.VMEM((tall, width), jnp.float32),
+            pltpu.VMEM((tile_rows, width), jnp.float32),
+            pltpu.VMEM((2 * rank, rows), jnp.float32),
+            pltpu.VMEM((n, 2 * rank, rows), jnp.float32),
+            pltpu.SemaphoreType.DMA((n,)),
+            pltpu.SemaphoreType.DMA((3, n)),
+            pltpu.SemaphoreType.DMA((3, n)),
+            pltpu.SemaphoreType.DMA((2, chips)),
+            pltpu.SemaphoreType.DMA((2, chips)),
+            pltpu.SemaphoreType.DMA((2, chips)),
+            pltpu.SemaphoreType.DMA((2, chips)),
+            pltpu.SemaphoreType.DMA((n,)),
+            pltpu.SemaphoreType.DMA((n,)),
+        ],
+        compiler_params=pltpu.CompilerParams(
+            collective_id=0, has_side_effects=True, vmem_limit_bytes=56 * 1024 * 1024
+        ),
+    )(
+        owners,
+        inputs,
+        base_weight,
+        cache_shrink.reshape(resident * rank, hidden),
+        cache_expand.reshape(resident * rank, width),
+        cache_magnitude.astype(jnp.float32),
+        select(store_shrink),
+        select(store_expand),
+        select(store_magnitude).astype(jnp.float32).reshape(n, 1, width),
+        row_mask,
+    )
+
+
+def fits_kernel(n, inputs, cache_shrink, cache_expand, tile_adapter):
+    rank = cache_shrink.shape[1]
+    rows = inputs.shape[0]
+    tile_rows = tile_adapter.shape[0] * rank
+    return (
+        n % 4 == 0
+        and cache_shrink.shape[2] % 128 == 0
+        and cache_expand.shape[2] % 128 == 0
+        and rank % 16 == 0
+        and rows == tile_rows
+        and rows % 128 == 0
+        and n * cache_shrink.shape[2] * cache_expand.shape[2] <= 2**23
+    )
+
+
+def local(n, *args):
+    if fits_kernel(n, args[0], args[2], args[3], args[8]):
+        return fused_local(n, *args)
+    return plain_local(*args)
+
+
 def solution(mesh):
     in_specs = (
         P("groups", "tensor"),
@@ -114,4 +587,5 @@
         P("groups"),
     )
     out_specs = P("groups", "tensor")
-    return jax.shard_map(local, mesh=mesh, in_specs=in_specs, out_specs=out_specs, check_vma=False)
+    body = functools.partial(local, mesh.shape["tensor"])
+    return jax.shard_map(body, mesh=mesh, in_specs=in_specs, out_specs=out_specs, check_vma=False)

time: 504 us -> 104 us (0.21); the launches traced: 495 us -> 103 us
  other arithmetic: 216 us -> 5.3 us
  local copies, waits for them, and re-layouts: 146 us -> 5.64 us
  Pallas kernels: 0 us -> 90.3 us
  blocking collectives: 62.8 us -> 0 us
  matrix products: 22.3 us -> 0 us
  starting transfers between devices: 19.3 us -> 0 us
  between operations: 16.1 us -> 1.96 us
  waiting for transfers between devices: 13.1 us -> 0 us
    unnamed x5 -> x0, other arithmetic: 204 us -> none
    pallas_call x0 -> x1, Pallas kernels: none -> 90.3 us  [fused_local(): pl.pallas_call(functools.partial(fused_kernel, n), out_shape=jax.ShapeDty...]
    all_to_all x6 -> x0, local copies, waits for them, and re-layouts: 83.5 us -> none  [the longest x2 62.1 us: local(): lax.all_to_all(sent_magnitude, 'tensor', split_axis=2, concat_axis=0, til...]
    psum x1 -> x0, blocking collectives: 62.8 us -> none  [local(): lax.psum((low_part, partial_gram_matrix, col_part), 'tensor')]
    unnamed x29 -> x3, local copies, waits for them, and re-layouts: 53.6 us -> 1.57 us
    dot_general x7 -> x0, matrix products: 22.3 us -> none  [the longest x1 9.83 us: local(): base_part = jnp.dot(inputs, base_weight, preferred_element_type=jnp.float32)]
    all_to_all x3 -> x0, starting transfers between devices: 19.1 us -> none  [the longest x1 7.6 us: local(): lax.all_to_all(sent_expand, 'tensor', split_axis=2, concat_axis=0, tiled=...]
    all_to_all x3 -> x0, waiting for transfers between devices: 13 us -> none  [the longest x1 13 us: local(): lax.all_to_all(sent_shrink, 'tensor', split_axis=2, concat_axis=0, tiled=...]
  transfers between devices with their start and end apart: 5 -> 0, of which waited for: 1 -> 0; matrix products, arithmetic and copies ran while one was open for 75% -> 0% of each run, Pallas kernels for 0% -> 0%
where the time goes in v1:
time: 104 us; the launch traced here: 103 us
  Pallas kernels  90.3 us (87%)
  local copies, waits for them, and re-layouts  5.64 us (5%)
  other arithmetic  5.3 us (5%)
  between operations  1.96 us (2%)
    pallas_call x1, Pallas kernels, fused_local(): pl.pallas_call(functools.partial(fused_kernel, n), out_shape=jax.ShapeDty...  90.3 us
    squeeze x2, local copies, waits for them, and re-layouts, select(): return lax.dynamic_index_in_dim(stored, chosen, 0, keepdims=False)  2.46 us

profile of v1, /device:TPU:0, one launch (start us, length us, event | category | flops | bytes accessed | tf_op | source)
XLA Modules:
  0.0 103.2 jit_solution(8888954714970581039)
XLA Ops:
  0.0 0.0 copy-start
  0.0 2.0 %fusion = (s32[]{:T(128)}, s32[4]{0:T(128)}) fusion(s32[]{:T(128)S(6)} %axis_index.12, s32[8]{0:T(128)} %param.18), kind=kLoop, calls=%fused_computation.10 | loop fusion | flops 87 | bytes 40 | tf_op jit(solution)/shard_map/reduce_sum | solution.py:490
  4.0 0.7 broadcast_in_dim.6
  4.7 0.1 eq.25
  4.8 1.3 %convert_element_type.19.cache_magnitude_ref = f32[4,512]{1,0:T(4,128)} convert(bf16[4,512]{1,0:T(4,128)(2,1)} %param.14) | non-fusion elementwise | flops 2048 | bytes 12288 | tf_op jit(solution)/shard_map/convert_element_type | solution.py:547
  6.1 0.8 constant_dynamic-slice_fusion
  6.9 0.6 convert.1.magnitude_ref
  7.5 1.4 %compare_convert_fusion.row_mask_ref = f32[128,128]{1,0:T(8,128)} fusion(s32[128]{0:T(128)} %param.19, s32[128]{0:T(128)S(1)} %eq.25), kind=kLoop, calls=%fused_computation.2 | loop fusion | flops 32768 | bytes 66560 | tf_op jit(solution)/shard_map/convert_element_type | solution.py:497
  8.9 1.7 %dynamic-slice_bitcast_fusion.1.expand_ref = bf16[16,8192]{1,0:T(8,128)(2,1)} fusion(bf16[2,16,8192]{2,1,0:T(8,128)(2,1)} %param.16, s32[]{:T(128)S(6)} %select_n.27), kind=kLoop, calls=%fused_computation.1 | loop fusion | bytes 524292 | tf_op jit(solution)/shard_map/jit(dynamic_index_in_dim)/squeeze | solution.py:495
  10.5 0.0 copy-done
  10.5 0.8 dynamic-slice_bitcast_fusion.shrink_ref
  11.3 90.3 %shard_map.100 = bf16[128,512]{1,0:T(8,128)(2,1)} custom-call(s32[4]{0:T(128)} %get-tuple-element.6.owners_ref, bf16[128,896]{1,0:T(8,128)(2,1)} %inputs_ref.1, bf16[896,8192]{1,0:T(8,128)(2,1)} %weight_ref.1, bf16[64,896]{1,0:T(8,128)(2,1)} %bitcast.9, bf16[64,512]{1,0:T(8,128)(2,1)} %bitcast.10, f32[4,512]{1,0:T(4,128)} %convert_element_type.19.cache_magnitude_ref, ...), custom_call_target="tpu_custom_call" | custom-call | tf_op jit(solution)/shard_map/pallas_call | solution.py:503
  101.6 1.6 %copy.12 = bf16[128,512]{1,0:T(8,128)(2,1)} copy(bf16[128,512]{1,0:T(8,128)(2,1)} %shard_map.100) | data formatting | bytes 262144
Async XLA Ops:
  0.0 10.5 %copy-start = (bf16[2,16,14336]{2,1,0:T(8,128)(2,1)S(1)}, bf16[2,16,14336]{2,1,0:T(8,128)(2,1)}, u32[]{:S(2)}) copy-start(bf16[2,16,14336]{2,1,0:T(8,128)(2,1)} %param.15) | copy-start | bytes 2752516

commit v2 on v1

--- a/solution.py
+++ b/solution.py
@@ -104,7 +104,8 @@
     )
 
 
-LAG = 4
+LAG = 3
+PARTS = 2
 MESH = pl.DeviceIdType.MESH
 
 
@@ -125,18 +126,24 @@
 
 def fused_kernel(
     n,
-    owners_ref,
+    tiles_ref,
     inputs_ref,
     weight_ref,
     cache_shrink_ref,
     cache_expand_ref,
     cache_magnitude_ref,
+    store_shrink_ref,
+    store_expand_ref,
+    store_magnitude_ref,
+    row_adapter_ref,
+    out_ref,
+    weight_buf,
+    store_shrink_buf,
+    store_expand_buf,
     shrink_ref,
     expand_ref,
     magnitude_ref,
     row_mask_ref,
-    out_ref,
-    weight_buf,
     got_shrink,
     got_expand,
     got_magnitude,
@@ -150,11 +157,10 @@
     cross_pair_in,
     cross_ring_out,
     cross_ring_in,
-    base_sum,
-    cross_sum,
     small_out,
     small_in,
     weight_sem,
+    store_sem,
     piece_send,
     piece_recv,
     pair_send,
@@ -185,10 +191,19 @@
     rows, hidden = inputs_ref.shape
     width = out_ref.shape[1]
     rank = shrink_ref.shape[0]
-    new = owners_ref.shape[0]
     resident_rows = cache_shrink_ref.shape[0]
     tile_rows = flat_shrink.shape[0]
     tiles = tile_rows // rank
+    resident = resident_rows // rank
+    new = tiles - resident
+    slots = store_shrink_ref.shape[0]
+    owners = [lax.div(tiles_ref[resident + t], slots) for t in range(new)]
+    store_copies = [
+        pltpu.make_async_copy(store_shrink_ref, store_shrink_buf, store_sem.at[0]),
+        pltpu.make_async_copy(store_expand_ref, store_expand_buf, store_sem.at[1]),
+    ]
+    for copy in store_copies:
+        copy.start()
 
     def weight_copy(slot):
         turn = lax.div(slot, 2)
@@ -219,6 +234,25 @@
         return carry
 
     lax.fori_loop(1, n, greet, 0)
+
+    chosen = jnp.int32(0)
+    for t in range(new):
+        chosen += jnp.where(owners[t] == me, lax.rem(tiles_ref[resident + t], slots), 0)
+    stored = store_magnitude_ref[...].astype(jnp.float32)
+    stored = jnp.sum(
+        jnp.where(lax.broadcasted_iota(jnp.int32, stored.shape, 0) == chosen, stored, 0.0),
+        axis=0,
+        keepdims=True,
+    )
+    for target in range(n):
+        magnitude_ref[target] = stored[:, target * width : (target + 1) * width]
+    for t in range(tiles):
+        same = (row_adapter_ref[...] == tiles_ref[t]).astype(jnp.float32)
+        row_mask_ref[pl.ds(t * rank, rank), :] = jnp.broadcast_to(same, (rank, rows))
+    for copy in store_copies:
+        copy.wait()
+    shrink_ref[...] = store_shrink_buf[chosen]
+    expand_ref[...] = store_expand_buf[chosen]
     pl.semaphore_wait(barrier, n - 1)
 
     def piece_parts(target):
@@ -278,13 +312,21 @@
             device_id_type=MESH,
         )
 
-    def ring_copy(chain, turn):
+    def part_rows(chain, part):
+        height = tile_rows if chain else rows
+        low, high = height * part // PARTS, height * (part + 1) // PARTS
+        if chain == 0 and part == PARTS - 1:
+            high = rows + 8
+        return pl.ds(low, high - low)
+
+    def ring_copy(chain, turn, part):
         source, landing = ((base_ring_out, base_ring_in), (cross_ring_out, cross_ring_in))[chain]
+        span = part_rows(chain, part)
         return pltpu.make_async_remote_copy(
-            src_ref=source.at[turn],
-            dst_ref=landing.at[turn],
-            send_sem=ring_send.at[chain, turn],
-            recv_sem=ring_recv.at[chain, turn],
+            src_ref=source.at[turn, span],
+            dst_ref=landing.at[turn, span],
+            send_sem=ring_send.at[chain, part, turn],
+            recv_sem=ring_recv.at[chain, part, turn],
             device_id={"tensor": following},
             device_id_type=MESH,
         )
@@ -322,35 +364,41 @@
         out[turn, pl.ds(0, rows if chain == 0 else tile_rows), :] = product(chain, slot)
         pair_copy(chain, turn).start()
 
-    def ring_turn(chain, turn):
+    def prepare(chain, turn):
         slot = 2 * turn + 1
-        total = (base_sum, cross_sum)[chain]
-        ring_out = (base_ring_out, cross_ring_out)[chain]
-        ring_in = (base_ring_in, cross_ring_in)[chain]
+        total = (base_ring_out, cross_ring_out)[chain]
         pair_in = (base_pair_in, cross_pair_in)[chain]
         if chain == 0:
             weight_copy(slot).wait()
-            total[pl.ds(rows, 8), :] = squares(slot)
-        total[pl.ds(0, rows if chain == 0 else tile_rows), :] = product(chain, slot)
+            own_squares = squares(slot)
+        own = product(chain, slot)
         pair_copy(chain, turn).wait_recv()
-        total[...] += pair_in[turn]
-
-        @pl.when(turn > 0)
-        def _():
-            ring_copy(chain, turn - 1).wait_recv()
-            total[...] += ring_in[turn - 1]
-
-        @pl.when(turn < chips - 1)
-        def _():
-            ring_out[turn] = total[...]
-            ring_copy(chain, turn).start()
+        height = own.shape[0]
+        total[turn, pl.ds(0, height), :] = own + pair_in[turn, pl.ds(0, height), :]
+        if chain == 0:
+            total[turn, pl.ds(rows, 8), :] = own_squares + pair_in[turn, pl.ds(rows, 8), :]
+
+    def ring_turn(chain, turn):
+        total = (base_ring_out, cross_ring_out)[chain]
+        ring_in = (base_ring_in, cross_ring_in)[chain]
+        for part in range(PARTS):
+            span = part_rows(chain, part)
+
+            @pl.when(turn > 0)
+            def _():
+                ring_copy(chain, turn - 1, part).wait_recv()
+                total[turn, span, :] += ring_in[turn - 1, span, :]
+
+            @pl.when(turn < chips - 1)
+            def _():
+                ring_copy(chain, turn, part).start()
 
     def adapters_ready():
         lax.fori_loop(0, n, piece_arrived, 0)
         flat_shrink[pl.ds(0, resident_rows), :] = cache_shrink_ref[...]
         flat_expand[pl.ds(0, resident_rows), :] = cache_expand_ref[...]
         for tile in range(new):
-            owner = owners_ref[tile]
+            owner = owners[tile]
             target = pl.ds(resident_rows + tile * rank, rank)
             flat_shrink[target, :] = got_shrink[owner]
             flat_expand[target, :] = got_expand[owner]
@@ -378,32 +426,42 @@
         second = lax.broadcasted_iota(jnp.int32, shape, 1) // rank
         return first == second
 
-    to_partner(0, 0)
     for copy in own_pieces():
         copy.start()
     lax.fori_loop(1, n, start_pieces, 0)
+    to_partner(0, 0)
+    to_partner(0, 1)
+    prepare(0, 0)
 
     def turn_body(turn, carry):
-        @pl.when(turn < chips - 1)
-        def _():
-            to_partner(0, turn + 1)
-
         @pl.when(turn < chips)
         def _():
             ring_turn(0, turn)
+
+        @pl.when(turn >= LAG)
+        def _():
+            ring_turn(1, turn - LAG)
+
+        @pl.when(turn < chips - 2)
+        def _():
+            to_partner(0, turn + 2)
+
+        @pl.when(turn < chips - 1)
+        def _():
+            prepare(0, turn + 1)
 
         @pl.when(turn == LAG - 1)
         def _():
             adapters_ready()
             to_partner(1, 0)
 
-        @pl.when((turn >= LAG) & (turn < chips + LAG - 1))
+        @pl.when((turn >= LAG - 1) & (turn < chips + LAG - 2))
         def _():
-            to_partner(1, turn - LAG + 1)
-
-        @pl.when(turn >= LAG)
+            to_partner(1, turn - LAG + 2)
+
+        @pl.when((turn >= LAG - 1) & (turn < chips + LAG - 1))
         def _():
-            ring_turn(1, turn - LAG)
+            prepare(1, turn - LAG + 1)
 
         return carry
 
@@ -423,12 +481,12 @@
     wide = expand.astype(jnp.float32)
     quadratic = exact_dot(gram, expand, ((1,), (0,)))
     change = jnp.sum(
-        (wide * (cross_sum[...] + quadratic)).reshape(tiles, rank, width), axis=1
-    )
-    column_squares = jnp.sum(base_sum[pl.ds(rows, 8), :], axis=0, keepdims=True)
+        (wide * (cross_ring_out[chips - 1] + quadratic)).reshape(tiles, rank, width), axis=1
+    )
+    column_squares = jnp.sum(base_ring_out[chips - 1, pl.ds(rows, 8), :], axis=0, keepdims=True)
     squared_norm = column_squares + 2.0 * ADAPTER_SCALING * change
     magnitude = jnp.concatenate(
-        [cache_magnitude_ref[...]] + [got_magnitude[owners_ref[t]] for t in range(new)], 0
+        [cache_magnitude_ref[...].astype(jnp.float32)] + [got_magnitude[owners[t]] for t in range(new)], 0
     )
     factor = magnitude / jnp.sqrt(squared_norm)
     row_mask = row_mask_ref[...]
@@ -442,7 +500,7 @@
         )
         for part in reversed(split3(spread))
     )
-    base = base_sum[pl.ds(0, rows), :]
+    base = base_ring_out[chips - 1, pl.ds(0, rows), :]
     out_ref[...] = (multiplier * (base + ADAPTER_SCALING * update)).astype(out_ref.dtype)
 
     lax.fori_loop(1, n, piece_sent, 0)
@@ -459,7 +517,8 @@
 
             @pl.when(turn < chips - 1)
             def _():
-                ring_copy(chain, turn).wait_send()
+                for part in range(PARTS):
+                    ring_copy(chain, turn, part).wait_send()
 
         return carry
 
@@ -479,35 +538,33 @@
     tile_adapter,
     row_adapter,
 ):
-    position = lax.axis_index("tensor")
-    slot_count, rank, _ = store_shrink.shape
+    slot_count, rank, all_hidden = store_shrink.shape
+    all_width = store_expand.shape[2]
     resident, _, hidden = cache_shrink.shape
     width = cache_expand.shape[2]
     rows = inputs.shape[0]
     tiles = tile_adapter.shape[0]
     tile_rows = tiles * rank
-    owners = tile_adapter[resident:] // slot_count
-    chosen = jnp.sum(
-        jnp.where(owners == position, tile_adapter[resident:] % slot_count, 0)
-    )
-
-    def select(stored):
-        return lax.dynamic_index_in_dim(stored, chosen, 0, keepdims=False)
-
-    row_mask = (jnp.repeat(tile_adapter, rank)[:, None] == row_adapter[None, :]).astype(
-        jnp.float32
-    )
     chips = n // 2
     tall = rows + 8
     vmem = pl.BlockSpec(memory_space=pltpu.VMEM)
+    hbm = pl.BlockSpec(memory_space=pl.ANY)
     return pl.pallas_call(
         functools.partial(fused_kernel, n),
         out_shape=jax.ShapeDtypeStruct((rows, width), jnp.bfloat16),
-        in_specs=[pl.BlockSpec(memory_space=pltpu.SMEM), vmem, pl.BlockSpec(memory_space=pl.ANY)]
-        + [vmem] * 7,
+        in_specs=[pl.BlockSpec(memory_space=pltpu.SMEM), vmem, hbm]
+        + [vmem] * 3
+        + [hbm] * 2
+        + [vmem] * 2,
         out_specs=vmem,
         scratch_shapes=[
             pltpu.VMEM((n, hidden, width), jnp.bfloat16),
+            pltpu.VMEM((slot_count, rank, all_hidden), jnp.bfloat16),
+            pltpu.VMEM((slot_count, rank, all_width), jnp.bfloat16),
+            pltpu.VMEM((rank, all_hidden), jnp.bfloat16),
+            pltpu.VMEM((rank, all_width), jnp.bfloat16),
+            pltpu.VMEM((n, 1, width), jnp.float32),
+            pltpu.VMEM((tile_rows, rows), jnp.float32),
             pltpu.VMEM((n, rank, hidden), jnp.bfloat16),
             pltpu.VMEM((n, rank, width), jnp.bfloat16),
             pltpu.VMEM((n, 1, width), jnp.float32),
@@ -515,23 +572,22 @@
             pltpu.VMEM((tile_rows, width), jnp.bfloat16),
             pltpu.VMEM((chips, tall, width), jnp.float32),
             pltpu.VMEM((chips, tall, width), jnp.float32),
-            pltpu.VMEM((chips - 1, tall, width), jnp.float32),
+            pltpu.VMEM((chips, tall, width), jnp.float32),
             pltpu.VMEM((chips - 1, tall, width), jnp.float32),
             pltpu.VMEM((chips, tile_rows, width), jnp.float32),
             pltpu.VMEM((chips, tile_rows, width), jnp.float32),
+            pltpu.VMEM((chips, tile_rows, width), jnp.float32),
             pltpu.VMEM((chips - 1, tile_rows, width), jnp.float32),
-            pltpu.VMEM((chips - 1, tile_rows, width), jnp.float32),
-            pltpu.VMEM((tall, width), jnp.float32),
-            pltpu.VMEM((tile_rows, width), jnp.float32),
             pltpu.VMEM((2 * rank, rows), jnp.float32),
             pltpu.VMEM((n, 2 * rank, rows), jnp.float32),
             pltpu.SemaphoreType.DMA((n,)),
+            pltpu.SemaphoreType.DMA((2,)),
             pltpu.SemaphoreType.DMA((3, n)),
             pltpu.SemaphoreType.DMA((3, n)),
             pltpu.SemaphoreType.DMA((2, chips)),
             pltpu.SemaphoreType.DMA((2, chips)),
-            pltpu.SemaphoreType.DMA((2, chips)),
-            pltpu.SemaphoreType.DMA((2, chips)),
+            pltpu.SemaphoreType.DMA((2, PARTS, chips)),
+            pltpu.SemaphoreType.DMA((2, PARTS, chips)),
             pltpu.SemaphoreType.DMA((n,)),
             pltpu.SemaphoreType.DMA((n,)),
         ],
@@ -539,16 +595,16 @@
             collective_id=0, has_side_effects=True, vmem_limit_bytes=56 * 1024 * 1024
         ),
     )(
-        owners,
+        tile_adapter,
         inputs,
         base_weight,
         cache_shrink.reshape(resident * rank, hidden),
         cache_expand.reshape(resident * rank, width),
-        cache_magnitude.astype(jnp.float32),
-        select(store_shrink),
-        select(store_expand),
-        select(store_magnitude).astype(jnp.float32).reshape(n, 1, width),
-        row_mask,
+        cache_magnitude,
+        store_shrink,
+        store_expand,
+        store_magnitude,
+        row_adapter.reshape(1, rows),
     )
 
 

time: 104 us -> 78.8 us (0.76)
  Pallas kernels: 90.3 us -> 77.1 us
  other arithmetic: 5.3 us -> 0 us
  local copies, waits for them, and re-layouts: 5.64 us -> 1.57 us
  between operations: 1.96 us -> 0.01 us
    pallas_call x1, Pallas kernels: 90.3 us -> 77.1 us  [fused_local(): pl.pallas_call(functools.partial(fused_kernel, n), out_shape=jax.ShapeDty...]
    convert_element_type x3 -> x0, other arithmetic: 3.29 us -> none  [the longest x1 1.37 us: fused_local(): (jnp.repeat(tile_adapter, rank)[:, None] == row_adapter[None, :]).astype(...]
    squeeze x2 -> x0, local copies, waits for them, and re-layouts: 2.46 us -> none  [select(): return lax.dynamic_index_in_dim(stored, chosen, 0, keepdims=False)]
    reduce_sum x1 -> x0, other arithmetic: 2.02 us -> none  [fused_local(): jnp.sum(jnp.where(owners == position, tile_adapter[resident:] % slot_coun...]
where the time goes in v2:
time: 78.8 us; the launch traced here: 78.7 us
  Pallas kernels  77.1 us (98%)
  local copies, waits for them, and re-layouts  1.57 us (2%)
    pallas_call x1, Pallas kernels, fused_local(): pl.pallas_call(functools.partial(fused_kernel, n), out_shape=jax.ShapeDty...  77.1 us

profile of v2, /device:TPU:0, one launch (start us, length us, event | category | flops | bytes accessed | tf_op | source)
XLA Modules:
  0.0 78.7 jit_solution(12026508278556933380)
XLA Ops:
  0.0 77.1 %shard_map.100 = bf16[128,512]{1,0:T(8,128)(2,1)} custom-call(s32[8]{0:T(128)} %tiles_ref.1, bf16[128,896]{1,0:T(8,128)(2,1)} %inputs_ref.1, bf16[896,8192]{1,0:T(8,128)(2,1)} %weight_ref.1, bf16[64,896]{1,0:T(8,128)(2,1)} %bitcast.3, bf16[64,512]{1,0:T(8,128)(2,1)} %bitcast.4, bf16[4,512]{1,0:T(4,128)(2,1)} %cache_magnitude_ref.1, ...), custom_call_target="tpu_custom_call" | custom-call | tf_op jit(solution)/shard_map/pallas_call | solution.py:552
  77.1 1.6 %copy.12 = bf16[128,512]{1,0:T(8,128)(2,1)} copy(bf16[128,512]{1,0:T(8,128)(2,1)} %shard_map.100) | data formatting | bytes 262144

commit v3 on v2

--- a/solution.py
+++ b/solution.py
@@ -104,8 +104,8 @@
     )
 
 
-LAG = 3
-PARTS = 2
+LAG = 1
+PARTS = 4
 MESH = pl.DeviceIdType.MESH
 
 
@@ -264,7 +264,7 @@
             (magnitude_ref.at[target], got_magnitude),
         )
 
-    def piece_copies(offset):
+    def piece_copies(offset, kinds=(0, 1, 2)):
         target = lax.rem(me + offset, n)
         return [
             pltpu.make_async_remote_copy(
@@ -276,10 +276,16 @@
                 device_id_type=MESH,
             )
             for kind, (source, landing) in enumerate(piece_parts(target))
+            if kind in kinds
         ]
 
-    def start_pieces(offset, carry):
-        for copy in piece_copies(offset):
+    def start_shrink(offset, carry):
+        for copy in piece_copies(offset, (0,)):
+            copy.start()
+        return carry
+
+    def start_others(offset, carry):
+        for copy in piece_copies(offset, (1, 2)):
             copy.start()
         return carry
 
@@ -294,11 +300,19 @@
             for kind, (source, landing) in enumerate(piece_parts(me))
         ]
 
-    def piece_arrived(sender, carry):
-        for kind, landing in enumerate((got_shrink, got_expand, got_magnitude)):
-            pltpu.make_async_copy(
-                landing.at[sender], landing.at[sender], piece_recv.at[kind, sender]
-            ).wait()
+    def landed(kind, sender):
+        landing = (got_shrink, got_expand, got_magnitude)[kind]
+        pltpu.make_async_copy(
+            landing.at[sender], landing.at[sender], piece_recv.at[kind, sender]
+        ).wait()
+
+    def shrink_arrived(sender, carry):
+        landed(0, sender)
+        return carry
+
+    def others_arrived(sender, carry):
+        landed(1, sender)
+        landed(2, sender)
         return carry
 
     def pair_copy(chain, turn):
@@ -394,14 +408,12 @@
                 ring_copy(chain, turn, part).start()
 
     def adapters_ready():
-        lax.fori_loop(0, n, piece_arrived, 0)
+        lax.fori_loop(0, n, shrink_arrived, 0)
         flat_shrink[pl.ds(0, resident_rows), :] = cache_shrink_ref[...]
-        flat_expand[pl.ds(0, resident_rows), :] = cache_expand_ref[...]
         for tile in range(new):
             owner = owners[tile]
             target = pl.ds(resident_rows + tile * rank, rank)
             flat_shrink[target, :] = got_shrink[owner]
-            flat_expand[target, :] = got_expand[owner]
         shrink = flat_shrink[...]
         contract = (((1,), (1,)), ((), ()))
         low = lax.dot_general(
@@ -419,6 +431,7 @@
             return carry
 
         lax.fori_loop(1, n, send, 0)
+        lax.fori_loop(1, n, start_others, 0)
 
     def tile_mask():
         shape = (tile_rows, tile_rows)
@@ -428,7 +441,7 @@
 
     for copy in own_pieces():
         copy.start()
-    lax.fori_loop(1, n, start_pieces, 0)
+    lax.fori_loop(1, n, start_shrink, 0)
     to_partner(0, 0)
     to_partner(0, 1)
     prepare(0, 0)
@@ -477,6 +490,10 @@
     small = lax.fori_loop(1, n, add_small, small_out[...])
     low = jnp.concatenate([small[:rank]] * tiles, 0)
     gram = jnp.where(tile_mask(), jnp.concatenate([small[rank:]] * tiles, 0), 0.0)
+    lax.fori_loop(0, n, others_arrived, 0)
+    flat_expand[pl.ds(0, resident_rows), :] = cache_expand_ref[...]
+    for tile in range(new):
+        flat_expand[pl.ds(resident_rows + tile * rank, rank), :] = got_expand[owners[tile]]
     expand = flat_expand[...]
     wide = expand.astype(jnp.float32)
     quadratic = exact_dot(gram, expand, ((1,), (0,)))

time: 78.8 us -> 76.7 us (0.973)
  Pallas kernels: 77.1 us -> 74.2 us
    pallas_call x1, Pallas kernels: 77.1 us -> 74.2 us  [fused_local(): pl.pallas_call(functools.partial(fused_kernel, n), out_shape=jax.ShapeDty...]
where the time goes in v3:
time: 76.7 us; the launch traced here: 75.8 us
  Pallas kernels  74.2 us (97%)
  local copies, waits for them, and re-layouts  1.57 us (2%)
    pallas_call x1, Pallas kernels, fused_local(): pl.pallas_call(functools.partial(fused_kernel, n), out_shape=jax.ShapeDty...  74.2 us
    unnamed x1, local copies, waits for them, and re-layouts  1.57 us

profile of v3, /device:TPU:0, one launch (start us, length us, event | category | flops | bytes accessed | tf_op | source)
XLA Modules:
  0.0 75.8 jit_solution(12125262335328943945)
XLA Ops:
  0.0 74.2 %shard_map.100 = bf16[128,512]{1,0:T(8,128)(2,1)} custom-call(s32[8]{0:T(128)} %tiles_ref.1, bf16[128,896]{1,0:T(8,128)(2,1)} %inputs_ref.1, bf16[896,8192]{1,0:T(8,128)(2,1)} %weight_ref.1, bf16[64,896]{1,0:T(8,128)(2,1)} %bitcast.3, bf16[64,512]{1,0:T(8,128)(2,1)} %bitcast.4, bf16[4,512]{1,0:T(4,128)(2,1)} %cache_magnitude_ref.1, ...), custom_call_target="tpu_custom_call" | custom-call | tf_op jit(solution)/shard_map/pallas_call | solution.py:569
  74.2 1.6 %copy.12 = bf16[128,512]{1,0:T(8,128)(2,1)} copy(bf16[128,512]{1,0:T(8,128)(2,1)} %shard_map.100) | data formatting | bytes 262144
